TPU v7x, 256 devices: a whole 4x4x8 slice. The times are simulated.
256 devices in a mesh: node: 32 (over y, z), local: 8 (over x, core).
Axes of the slice: x: 4, y: 4, z: 8, core: 2. Of those that a mesh axis runs over, the one named last changes fastest.
Arguments:
- tokens: bfloat16 [4096, 7168], P('node', 'local'), may hold values from -6 to 6
- routes: int32 [4096, 8], P('node'), may hold values from 0 to 63, as said below
- gates: bfloat16 [4096, 8], P('node'), may hold values from 0.099609375 to 0.69921875
- w_gate: bfloat16 [256, 7168, 256], P(('node', 'local')), may hold values from -0.0625 to 0.0625
- w_up: bfloat16 [256, 7168, 256], P(('node', 'local')), may hold values from -0.0625 to 0.0625
- w_down: bfloat16 [256, 256, 7168], P(('node', 'local')), may hold values from -0.1875 to 0.1875
Outputs:
- mixed: bfloat16 [4096, 7168], P('node', 'local')
Inputs may be any that keep to these rules, and one draw needn't show every extreme that they name: `routes`: each token names 8 different experts: all 2 experts of each of 4 different nodes, the node of expert e being e // 2, in any order. In each aligned block of 128 tokens no node is named by more than 24 tokens, and one node is named by exactly 24 tokens of every block.
All inputs are finite; a program needn't handle non-finite values.
Results may differ from a plain program's by a relative error of at most 0.02.
Values may be sent and summed in bfloat16 or wider, within the bound.
A program may use at most 128 MiB of HBM per device.

v0:
```python
import jax
import jax.numpy as jnp
from jax import lax
from jax.sharding import PartitionSpec as P

EXP_NODE = 2


def on_device(tokens, routes, gates, w_gate, w_up, w_down):
    tok_rows, feat_width = tokens.shape
    node_count = lax.axis_size("node")
    local_count = lax.axis_size("local")
    split_count = local_count // EXP_NODE
    capacity = 6 * tok_rows // node_count
    slot_count = node_count * capacity
    expert_ids = jnp.arange(node_count * EXP_NODE, dtype=jnp.int32)
    matches = routes[:, :, None] == expert_ids[None, None, :]
    weight = jnp.sum(
        jnp.where(matches, gates[:, :, None].astype(jnp.float32), jnp.float32(0.0)), axis=1
    )
    hit_counts = jnp.sum(matches.astype(jnp.int32), axis=1)
    node_hits = jnp.sum(hit_counts.reshape(tok_rows, node_count, EXP_NODE), axis=2)
    named = (node_hits > 0).astype(jnp.int32)
    earlier = jnp.cumsum(named, axis=0) - named
    slot_ids = jnp.arange(capacity, dtype=jnp.int32)
    placed = (named.T[:, None, :] > 0) & (earlier.T[:, None, :] == slot_ids[None, :, None])
    placed_rows = placed.astype(jnp.bfloat16).reshape(slot_count, tok_rows)
    weight_nodes = weight.reshape(tok_rows, node_count, EXP_NODE).transpose(1, 0, 2)
    slot_gates = jnp.sum(
        jnp.where(placed[:, :, :, None], weight_nodes[:, None, :, :], jnp.float32(0.0)), axis=2
    )
    slot_gates = slot_gates.reshape(slot_count, EXP_NODE).astype(jnp.bfloat16)
    gate_slab = w_gate[0]
    up_slab = w_up[0]
    full_rows = lax.all_gather(tokens, "local", axis=1, tiled=True)
    outgoing = jnp.dot(placed_rows, full_rows, preferred_element_type=jnp.float32).astype(
        jnp.bfloat16
    )
    rows_in, gates_in = (
        lax.all_to_all(outgoing, "node", split_axis=0, concat_axis=0, tiled=True),
        lax.all_to_all(slot_gates, "node", split_axis=0, concat_axis=0, tiled=True),
    )
    gate_act = jnp.dot(rows_in, gate_slab, preferred_element_type=jnp.float32)
    up_act = jnp.dot(rows_in, up_slab, preferred_element_type=jnp.float32)
    own_group = lax.axis_index("local") // split_count
    own_gate = lax.dynamic_slice_in_dim(gates_in, own_group, 1, 1).astype(jnp.float32)
    hidden = (jax.nn.silu(gate_act) * up_act * own_gate).astype(jnp.bfloat16)
    down_rows = w_down[0]
    node_sum = lax.psum_scatter(
        lax.dot_general(
            down_rows, hidden, (((0,), (1,)), ((), ())), preferred_element_type=jnp.float32
        ).astype(jnp.bfloat16),
        "local",
        scatter_dimension=0,
        tiled=True,
    )
    returned = lax.all_to_all(node_sum, "node", split_axis=1, concat_axis=1, tiled=True)
    mixed = lax.dot_general(
        placed_rows, returned, (((0,), (1,)), ((), ())), preferred_element_type=jnp.float32
    )
    return mixed.astype(jnp.bfloat16)


def solution(mesh):
    return jax.shard_map(
        on_device,
        mesh=mesh,
        in_specs=(
            P("node", "local"),
            P("node", None),
            P("node", None),
            P(("node", "local"), None, None),
            P(("node", "local"), None, None),
            P(("node", "local"), None, None),
        ),
        out_specs=P("node", "local"),
        check_vma=False,
    )
```

profile of v0, /device:TPU:1, one launch (start us, length us, event | category | flops | bytes accessed | tf_op | source)
XLA Modules:
  0.0 476.5 jit_solution(8043706405143563685)
XLA Ops:
  6.5 0.7 all-gather.2.cloned.1.call-update
  7.3 0.7 convert_element_type.37
  7.9 0.7 convert_reduce_fusion
  8.7 0.1 copy.32
  8.8 0.1 copy.33
  8.9 0.2 reduce_window_sum.11
  9.2 0.7 select_reduce_fusion.1
  9.9 0.1 fusion.25
  10.0 0.9 select_reduce_fusion
  10.9 12.0 %all-to-all-start.1 = ((bf16[32,24,2]{1,2,0:T(2,128)(2,1)}), bf16[32,24,2]{1,2,0:T(2,128)(2,1)S(1)}, u32[]{:S(2)}, u32[]{:S(2)}) async-start(bf16[32,24,2]{1,2,0:T(2,128)(2,1)} %select_reduce_fusion), calls=%async_computation.1 | async-start | bytes 32768 | tf_op jit(solution)/shard_map/all_to_all | solution.py:41
  23.0 0.1 eq.49
  23.1 0.2 fusion.26
  23.3 17.8 %all-gather.2.cloned.1.call-done = bf16[128,7168]{1,0:T(8,128)(2,1)} async-done(((bf16[128,896]{1,0:T(8,128)(2,1)}), bf16[128,7168]{1,0:T(8,128)(2,1)}) %all-gather.2.cloned.1.call-update) | async-done | bytes 1835024 | tf_op jit(solution)/shard_map/all_gather | solution.py:35
  41.0 7.1 %convolution_convert_fusion.1 = bf16[768,7168]{1,0:T(8,128)(2,1)} fusion(pred[768,128]{1,0:T(32,128)(4,1)S(1)} %fusion.26, bf16[128,7168]{1,0:T(8,128)(2,1)} %all-gather.2.cloned.1.call-done), kind=kOutput, calls=%fused_computation.1 | convolution fusion | flops 1414791168 | bytes 12943360 | tf_op jit(solution)/shard_map/dot_general | solution.py:36
  48.2 9.7 %all-to-all-start = ((bf16[32,24,7168]{2,1,0:T(8,128)(2,1)}), bf16[32,24,7168]{2,1,0:T(8,128)(2,1)}, u32[]{:S(2)}, u32[]{:S(2)}) async-start(bf16[32,24,7168]{2,1,0:T(8,128)(2,1)} %bitcast.48), calls=%async_computation | async-start | bytes 22020096 | tf_op jit(solution)/shard_map/all_to_all | solution.py:40
  57.9 0.1 all_to_all.24
  58.1 245.4 %all-to-all-done = bf16[32,24,7168]{2,1,0:T(8,128)(2,1)} async-done(((bf16[32,24,7168]{2,1,0:T(8,128)(2,1)}), bf16[32,24,7168]{2,1,0:T(8,128)(2,1)}, u32[]{:S(2)}, u32[]{:S(2)}) %all-to-all-start) | async-done | bytes 11010080 | tf_op jit(solution)/shard_map/all_to_all | solution.py:40
  303.5 6.9 %fusion.4 = f32[768,256]{1,0:T(8,128)S(1)} fusion(bf16[768,7168]{1,0:T(8,128)(2,1)} %bitcast.6, bf16[1,7168,256]{2,1,0:T(8,128)(2,1)} %param.9), kind=kOutput, calls=%fused_computation.6 | convolution fusion | flops 2818572288 | bytes 15466496 | tf_op jit(solution)/shard_map/dot_general | solution.py:43
  310.4 18.9 %fusion = bf16[7168,768]{0,1:T(8,128)(2,1)} fusion(bf16[1,256,7168]{2,1,0:T(8,128)(2,1)} %param.11, bf16[768,7168]{1,0:T(8,128)(2,1)} %bitcast.6, bf16[1,7168,256]{2,1,0:T(8,128)(2,1)} %param.10, f32[768,256]{1,0:T(8,128)S(1)} %fusion.4, f32[768]{0:T(1024)S(1)} %convert_reduce_fusion.1), kind=kOutput, calls=%fused_computation.2 | convolution fusion | flops 5644025856 | bytes 30149632 | tf_op jit(solution)/shard_map/dot_general | solution.py:50
  329.2 14.7 %copy.36 = bf16[7168,768]{1,0:T(8,128)(2,1)} copy(bf16[7168,768]{0,1:T(8,128)(2,1)} %fusion) | data formatting | bytes 22020096
  344.0 80.9 %reduce-scatter.4.cloned.1.call-done = bf16[896,768]{1,0:T(8,128)(2,1)} async-done(((bf16[7168,768]{1,0:T(8,128)(2,1)}), bf16[896,768]{1,0:T(8,128)(2,1)}) %reduce-scatter.4.cloned.1.call-update) | async-done | bytes 1376272
  424.9 1.8 copy.37
  426.7 41.9 %all_to_all.30 = bf16[896,32,24]{0,2,1:T(8,128)(2,1)S(1)} all-to-all(bf16[896,32,24]{0,2,1:T(8,128)(2,1)S(1)} %bitcast.49), channel_id=1, replica_groups=mesh['node'=32,'local'=8] {'node'}, dimensions={1} | all-to-all | bytes 2752512 | tf_op jit(solution)/shard_map/all_to_all | solution.py:57
  468.5 1.1 fusion.17
  (11 shorter events, 0.2 us)
Async XLA Ops:
  6.5 34.5 %all-gather.2.cloned.1.call-start = ((), (), s32[]{:S(2)}) async-start(), calls=%async_computation.4 | async-start | bytes 2064384 | tf_op jit(solution)/shard_map/all_gather | solution.py:35
  10.9 37.2 %all-to-all-start.1 = ((bf16[32,24,2]{1,2,0:T(2,128)(2,1)}), bf16[32,24,2]{1,2,0:T(2,128)(2,1)S(1)}, u32[]{:S(2)}, u32[]{:S(2)}) async-start(bf16[32,24,2]{1,2,0:T(2,128)(2,1)} %select_reduce_fusion), calls=%async_computation.1 | async-start | bytes 32768 | tf_op jit(solution)/shard_map/all_to_all | solution.py:41
  48.2 255.3 %all-to-all-start = ((bf16[32,24,7168]{2,1,0:T(8,128)(2,1)}), bf16[32,24,7168]{2,1,0:T(8,128)(2,1)}, u32[]{:S(2)}, u32[]{:S(2)}) async-start(bf16[32,24,7168]{2,1,0:T(8,128)(2,1)} %bitcast.48), calls=%async_computation | async-start | bytes 22020096 | tf_op jit(solution)/shard_map/all_to_all | solution.py:40
  57.9 367.0 %reduce-scatter.4.cloned.1.call-start = ((), (), s32[]{:S(2)}) async-start(), calls=%async_computation.5 | async-start | bytes 12386304
Sparse Core Ops, SparseCore 0:
  9.2 31.8 all-gather.1
  344.1 80.7 reduce-scatter.3
where the time goes:
time: 480 us; the launch traced here: 476 us
  waiting for transfers between devices  345 us (72%)
  blocking collectives  41.9 us (9%)
  matrix products  34 us (7%)
  starting transfers between devices  21.8 us (5%)
  local copies, waits for them, and re-layouts  16.9 us (4%)
  between operations  13.5 us (3%)
    all_to_all x1, waiting for transfers between devices, on_device(): lax.all_to_all(outgoing, 'node', split_axis=0, concat_axis=0, tiled=True)  245 us
    unnamed x3, waiting for transfers between devices  81.6 us
    all_to_all x1, blocking collectives, on_device(): lax.all_to_all(node_sum, 'node', split_axis=1, concat_axis=1, tiled=True)  41.9 us
    dot_general x1, matrix products, on_device(): lax.dot_general(down_rows, hidden, (((0,), (1,)), ((), ())), preferred_el...  18.9 us
    all_gather x1, waiting for transfers between devices, on_device(): full_rows = lax.all_gather(tokens, 'local', axis=1, tiled=True)  17.8 us
    unnamed x2, local copies, waits for them, and re-layouts  16.5 us
    all_to_all x1, starting transfers between devices, on_device(): lax.all_to_all(slot_gates, 'node', split_axis=0, concat_axis=0, tiled=True)  12 us
    all_to_all x1, starting transfers between devices, on_device(): lax.all_to_all(outgoing, 'node', split_axis=0, concat_axis=0, tiled=True)  9.69 us
  transfers between devices with their start and end apart: 4, of which 3 were waited for; matrix products, arithmetic and copies ran while one was open for 2% of the time, Pallas kernels for 0%

commit v1 on v0

v1 whole, which is shorter than its diff:
```python
import jax
import jax.numpy as jnp
from jax import lax
from jax.experimental import pallas as pl
from jax.experimental.pallas import tpu as pltpu
from jax.sharding import PartitionSpec as P

F32, BF16 = jnp.float32, jnp.bfloat16
NY, NZ, NX = 4, 8, 4
TOK = 128
FEAT = 896
WIDTH = 256
DEPTH = FEAT * 8
CAP = 24
PAIR = 2 * CAP
ROWS = NY * PAIR
EARLY = 0
MAIN = FEAT - EARLY
WIDE = MAIN + 4 * EARLY
GATE = 128
CHUNKS = ((0, 4), (3, 5), (2, 6), (1, 7))
SLOT = {0: 0, 4: 1, 3: 2, 5: 3, 2: 4, 6: 5, 1: 6, 7: 7}
OWN = GATE
SIB = GATE + WIDE
SIDE = GATE + 2 * WIDE
MISSING = -100.0


def kernel(
    tok, routes_t, gates_t, wg_h, wu_h, wd_h, out,
    zb, meta_out, meta_in, onehot, picked, rows, wg, wu, wd, hid, osend, ret, zso, zsi, own,
    send_sem, recv_sem, local_sem,
):
    node, local = lax.axis_index("node"), lax.axis_index("local")
    y, z, x, c = node // NZ, node % NZ, local // 2, local % 2

    def dev(dx=0, dc=0, dy=0, dz=0):
        yy, zz = (y + dy + NY) % NY, (z + dz + NZ) % NZ
        xx, cc = (x + dx + NX) % NX, (c + dc) % 2
        return (yy * NZ + zz, xx * 2 + cc)

    counts = {"remote": 0, "local": 0}
    remote_copies = []

    def remote(src, dst, device):
        i = counts["remote"]
        counts["remote"] += 1
        copy = pltpu.make_async_remote_copy(
            src_ref=src, dst_ref=dst, send_sem=send_sem.at[i], recv_sem=recv_sem.at[i],
            device_id=device, device_id_type=pl.DeviceIdType.MESH,
        )
        copy.start()
        remote_copies.append(copy)
        return copy

    def load(src, dst):
        i = counts["local"]
        counts["local"] += 1
        copy = pltpu.make_async_copy(src, dst, local_sem.at[i])
        copy.start()
        return copy

    toward = 1 - 2 * c

    own_tokens = load(tok, zb.at[pl.ds(0, TOK), pl.ds(0, FEAT)])
    peers = (
        [dev(dx=i, dc=j) for i in range(NX) for j in range(2) if (i, j) != (0, 0)]
        + [dev(dy=i) for i in range(1, NY)]
        + [dev(dz=i) for i in range(1, NZ)]
    )
    barrier = pltpu.get_barrier_semaphore()
    for peer in peers:
        pl.semaphore_signal(barrier, inc=1, device_id=peer, device_id_type=pl.DeviceIdType.MESH)

    lane = lax.broadcasted_iota(jnp.int32, (TOK, TOK), 1)
    line = lax.broadcasted_iota(jnp.int32, (TOK, TOK), 0)
    step, kind = line // 16, line % 16
    target = ((y + kind % NY) % NY) * NZ + (z + step) % NZ
    expert = target * 2 + x // 2
    named = jnp.zeros((TOK, TOK), F32)
    weight = jnp.zeros((TOK, TOK), F32)
    routes_v, gates_v = routes_t[...], gates_t[...].astype(F32)
    for k in range(8):
        chosen = routes_v[k : k + 1, :]
        named = jnp.where(chosen // 2 == target, 1.0, named)
        weight = weight + jnp.where(chosen == expert, gates_v[k : k + 1, :], 0.0)
    before = jnp.where(line < lane, 1.0, 0.0).astype(BF16)
    earlier = jnp.dot(named.astype(BF16), before, preferred_element_type=F32)
    slots = jnp.where(named > 0.0, earlier, MISSING)
    meta = jnp.where(kind < 4, slots, jnp.where(kind < 8, weight, 0.0)).astype(BF16)
    meta_out[...] = meta
    meta_in[pl.ds(0, 16), :] = meta[0:16]

    own_tokens.wait()
    pl.semaphore_wait(barrier, len(peers))

    def block(i):
        return zb.at[pl.ds(SLOT[i] * TOK, TOK), :]

    if EARLY:
        first = [
            remote(
                zb.at[pl.ds(0, TOK), pl.ds(MAIN, EARLY)],
                zb.at[pl.ds(0, TOK), pl.ds(FEAT + j * EARLY, EARLY)],
                dev(dx=dx),
            )
            for j, dx in enumerate((1, -1, 2))
        ]
        for copy in first:
            copy.wait_recv()
    arrive = {1: remote(block(0), block(1), dev(dz=1)), 7: remote(block(0), block(7), dev(dz=-1))}
    metas = {
        i: remote(
            meta_out.at[pl.ds(16 * i, 16), :], meta_in.at[pl.ds(16 * SLOT[i], 16), :], dev(dz=i)
        )
        for i in range(1, NZ)
    }

    def first_row(dx, dc):
        return (((x + dx + NX) % NX) * 2 + (c + dc) % 2) * FEAT

    def aligned(i):
        return pl.multiple_of(i, 128)

    pieces = []
    for dc in range(2):
        pieces.append((first_row(0, dc), dc * WIDE, FEAT))
        if EARLY:
            for j, dx in enumerate((-1, 1, 2)):
                pieces.append((first_row(dx, dc) + MAIN, dc * WIDE + FEAT + j * EARLY, EARLY))
    for j, dx in enumerate((-1, 1, 2)):
        for dc in range(2):
            pieces.append((first_row(dx, dc), 2 * WIDE + (2 * j + dc) * MAIN, MAIN))
    weight_loads = []
    for src, dst, size in pieces:
        for hbm, vmem in ((wg_h, wg), (wu_h, wu)):
            weight_loads.append(
                load(hbm.at[0, pl.ds(aligned(src), size), :], vmem.at[pl.ds(dst, size), :])
            )
    down_load = load(wd_h.at[0, :, pl.ds(aligned(first_row(0, 0)), FEAT)], wd.at[pl.ds(0, WIDTH), :])
    downs = []
    for dx, dc, place in ((0, 1, 1), (1, 0, 2), (1, 1, 3), (-1, 0, 4), (-1, 1, 5), (2, 0, 6), (2, 1, 7)):
        downs.append(
            remote(
                wd_h.at[0, :, pl.ds(aligned(first_row(dx, dc)), FEAT)],
                wd.at[pl.ds(place * WIDTH, WIDTH), :],
                dev(dx=dx, dc=dc),
            )
        )

    for i in (1, 2):
        arrive[i].wait_recv()
        arrive[i + 1] = remote(block(i), block(i + 1), dev(dz=1))
        arrive[8 - i].wait_recv()
        arrive[7 - i] = remote(block(8 - i), block(7 - i), dev(dz=-1))
    arrive[3].wait_recv()
    arrive[5].wait_recv()
    arrive[4] = remote(zb.at[pl.ds((SLOT[3] + c) * TOK, TOK), :], block(4), dev(dz=toward))
    for copy in metas.values():
        copy.wait_recv()

    to_node, row_copies, sib_copies = {}, {}, {}
    hid_copies, hid_sibs, to_home, z_copies = {}, {}, {}, {}

    def select(k):
        near, far = (meta_in[pl.ds(16 * (2 * k + i), 16), :].astype(F32) for i in range(2))
        place = lax.broadcasted_iota(jnp.int32, (PAIR, 2 * TOK), 0).astype(F32)
        for j in range(NY):
            slot = jnp.concatenate([near[j : j + 1], far[j : j + 1] + CAP], axis=1)
            gate = jnp.concatenate([near[4 + j : 5 + j], far[4 + j : 5 + j]], axis=1)
            hit = jnp.where(place == slot, 1.0, 0.0)
            onehot[k, pl.ds(j * PAIR, PAIR), :] = hit.astype(BF16)
            share = jnp.sum(hit * gate, axis=1, keepdims=True)
            picked[k, pl.ds(j * PAIR, PAIR), pl.ds(0, GATE)] = jnp.broadcast_to(
                share, (PAIR, GATE)
            ).astype(BF16)
        chosen = jnp.dot(
            onehot[k], zb[pl.ds(2 * k * TOK, 2 * TOK), :], preferred_element_type=F32
        ).astype(BF16)
        picked[k, :, pl.ds(GATE, WIDE)] = chosen
        to_node[k] = [
            remote(
                picked.at[k, pl.ds(j * PAIR, PAIR), :],
                rows.at[k, pl.ds(j * PAIR, PAIR), pl.ds(0, GATE + WIDE)],
                dev(dy=j),
            )
            for j in range(1, NY)
        ]
        rows[k, pl.ds(0, PAIR), pl.ds(0, GATE + WIDE)] = picked[k, pl.ds(0, PAIR), :]

    def cols(k, first, size):
        return rows.at[k, :, pl.ds(first, size)]

    def side(k, j, dc=0):
        return cols(k, SIDE + (2 * j + dc) * MAIN, MAIN)

    def rows_a(k):
        for copy in to_node[k]:
            copy.wait_recv()
        row_copies[k] = [
            remote(cols(k, OWN, MAIN), side(k, 0), dev(dx=1)),
            remote(cols(k, OWN, MAIN), side(k, 1), dev(dx=-1)),
        ]
        sib_copies[k] = [remote(cols(k, OWN, WIDE), cols(k, SIB, WIDE), dev(dc=1))]

    def rows_b(k):
        for j in range(2):
            row_copies[k][j].wait_recv()
        row_copies[k].append(
            remote(
                rows.at[k, :, pl.ds(aligned(SIDE + c * 2 * MAIN), MAIN)], side(k, 2), dev(dx=toward)
            )
        )
        for j in range(2):
            sib_copies[k].append(remote(side(k, j), side(k, j, 1), dev(dc=1)))

    def rows_c(k):
        row_copies[k][2].wait_recv()
        sib_copies[k].append(remote(side(k, 2), side(k, 2, 1), dev(dc=1)))

    def hcol(k, place):
        return hid.at[k, :, pl.ds(place * WIDTH, WIDTH)]

    def up(k):
        for copy in sib_copies[k]:
            copy.wait_recv()
        gate_act = jnp.dot(rows[k, :, pl.ds(GATE, DEPTH)], wg[...], preferred_element_type=F32)
        up_act = jnp.dot(rows[k, :, pl.ds(GATE, DEPTH)], wu[...], preferred_element_type=F32)
        share = rows[k, :, pl.ds(0, GATE)].astype(F32)
        share = jnp.concatenate([share, share], axis=1)
        value = gate_act / (1.0 + jnp.exp(-gate_act)) * up_act * share
        hid[k, :, pl.ds(0, WIDTH)] = value.astype(BF16)
        hid_copies[k] = [
            remote(hcol(k, 0), hcol(k, 2), dev(dx=1)),
            remote(hcol(k, 0), hcol(k, 4), dev(dx=-1)),
        ]
        hid_sibs[k] = [remote(hcol(k, 0), hcol(k, 1), dev(dc=1))]

    def hid_b(k):
        for j in range(2):
            hid_copies[k][j].wait_recv()
        hid_copies[k].append(
            remote(
                hid.at[k, :, pl.ds(aligned((2 + 2 * c) * WIDTH), WIDTH)], hcol(k, 6), dev(dx=toward)
            )
        )
        for j in range(2):
            hid_sibs[k].append(remote(hcol(k, 2 + 2 * j), hcol(k, 3 + 2 * j), dev(dc=1)))

    def hid_c(k):
        hid_copies[k][2].wait_recv()
        hid_sibs[k].append(remote(hcol(k, 6), hcol(k, 7), dev(dc=1)))

    def down(k):
        for copy in hid_sibs[k]:
            copy.wait_recv()
        osend[k] = jnp.dot(hid[k], wd[...], preferred_element_type=F32).astype(BF16)
        to_home[k] = [
            remote(
                osend.at[k, pl.ds(j * PAIR, PAIR), :], ret.at[k, pl.ds(j * PAIR, PAIR), :], dev(dy=-j)
            )
            for j in range(1, NY)
        ]
        ret[k, pl.ds(0, PAIR), :] = osend[k, pl.ds(0, PAIR), :]

    def home(k):
        for copy in to_home[k]:
            copy.wait_recv()
        total = lax.dot_general(
            onehot[k], ret[k], (((0,), (0,)), ((), ())), preferred_element_type=F32
        )
        near, far = total[:TOK], total[TOK:]
        if k == 0:
            own[...] = near
            zso[0] = far.astype(BF16)
            z_copies[0] = [remote(zso.at[0], zsi.at[0], dev(dz=-toward))]
            return
        for copy in z_copies[k - 1]:
            copy.wait_recv()
        if k == 1:
            come = zsi[0].astype(F32)
            near = near + jnp.where(c == 0, come, 0.0)
            far = far + jnp.where(c == 1, come, 0.0)
        else:
            near = near + zsi[2 * k - 3].astype(F32)
            far = far + zsi[2 * k - 2].astype(F32)
        zso[2 * k - 1] = near.astype(BF16)
        zso[2 * k] = far.astype(BF16)
        z_copies[k] = [
            remote(zso.at[2 * k - 1], zsi.at[2 * k - 1], dev(dz=-1)),
            remote(zso.at[2 * k], zsi.at[2 * k], dev(dz=1)),
        ]

    select(1)
    arrive[4].wait_recv()
    select(0)
    select(2)
    rows_a(0)
    select(3)
    rows_b(0)
    rows_a(1)
    rows_c(0)
    for copy in weight_loads:
        copy.wait()
    up(0)
    rows_b(1)
    rows_a(2)
    hid_b(0)
    rows_c(1)
    up(1)
    hid_c(0)
    rows_b(2)
    rows_a(3)
    hid_b(1)
    down_load.wait()
    for copy in downs:
        copy.wait_recv()
    down(0)
    rows_c(2)
    up(2)
    hid_c(1)
    home(0)
    rows_b(3)
    hid_b(2)
    down(1)
    rows_c(3)
    up(3)
    hid_c(2)
    home(1)
    hid_b(3)
    down(2)
    hid_c(3)
    home(2)
    down(3)
    home(3)
    for copy in z_copies[3]:
        copy.wait_recv()
    out[...] = (own[...] + zsi[5].astype(F32) + zsi[6].astype(F32)).astype(BF16)
    for copy in remote_copies:
        copy.wait_send()


REMOTE = (3 if EARLY else 0) + 7 + 7 + 7 + 4 * (3 + 7 + 7 + 3) + 7
LOCAL = 2 + 2 * (8 + (6 if EARLY else 0))


def on_device(tokens, routes, gates, w_gate, w_up, w_down):
    any_spec = pl.BlockSpec(memory_space=pl.ANY)
    vmem_spec = pl.BlockSpec(memory_space=pltpu.VMEM)
    return pl.pallas_call(
        kernel,
        name="routed_experts",
        out_shape=jax.ShapeDtypeStruct((TOK, FEAT), BF16),
        in_specs=[any_spec, vmem_spec, vmem_spec, any_spec, any_spec, any_spec],
        out_specs=vmem_spec,
        scratch_shapes=[
            pltpu.VMEM((NZ * TOK, WIDE), BF16),
            pltpu.VMEM((NZ * 16, TOK), BF16),
            pltpu.VMEM((NZ * 16, TOK), BF16),
            pltpu.VMEM((4, ROWS, 2 * TOK), BF16),
            pltpu.VMEM((4, ROWS, GATE + WIDE), BF16),
            pltpu.VMEM((4, ROWS, GATE + DEPTH), BF16),
            pltpu.VMEM((DEPTH, WIDTH), BF16),
            pltpu.VMEM((DEPTH, WIDTH), BF16),
            pltpu.VMEM((8 * WIDTH, FEAT), BF16),
            pltpu.VMEM((4, ROWS, 8 * WIDTH), BF16),
            pltpu.VMEM((4, ROWS, FEAT), BF16),
            pltpu.VMEM((4, ROWS, FEAT), BF16),
            pltpu.VMEM((7, TOK, FEAT), BF16),
            pltpu.VMEM((7, TOK, FEAT), BF16),
            pltpu.VMEM((TOK, FEAT), F32),
            pltpu.SemaphoreType.DMA((REMOTE,)),
            pltpu.SemaphoreType.DMA((REMOTE,)),
            pltpu.SemaphoreType.DMA((LOCAL,)),
        ],
        compiler_params=pltpu.CompilerParams(
            collective_id=0, has_side_effects=True, vmem_limit_bytes=56 << 20
        ),
        cost_estimate=pl.CostEstimate(
            flops=8_500_000_000, bytes_accessed=12_000_000, transcendentals=200_000
        ),
    )(tokens, routes.T, gates.T, w_gate, w_up, w_down)


def solution(mesh):
    return jax.shard_map(
        on_device,
        mesh=mesh,
        in_specs=(
            P("node", "local"),
            P("node", None),
            P("node", None),
            P(("node", "local"), None, None),
            P(("node", "local"), None, None),
            P(("node", "local"), None, None),
        ),
        out_specs=P("node", "local"),
        check_vma=False,
    )
```

time: 480 us -> 143 us (0.30)
  waiting for transfers between devices: 345 us -> 0 us
  Pallas kernels: 0 us -> 141 us
  blocking collectives: 41.9 us -> 0 us
  matrix products: 34 us -> 0 us
  starting transfers between devices: 21.8 us -> 0 us
  local copies, waits for them, and re-layouts: 16.9 us -> 1.65 us
  between operations: 13.5 us -> 0.01 us
    all_to_all x2 -> x0, waiting for transfers between devices: 245 us -> none  [the longest x1 245 us: on_device(): lax.all_to_all(outgoing, 'node', split_axis=0, concat_axis=0, tiled=True)]
    pallas_call x0 -> x1, Pallas kernels: none -> 141 us  [on_device(): pl.pallas_call(kernel, name='routed_experts', out_shape=jax.ShapeDtypeStr...]
    unnamed x3 -> x0, waiting for transfers between devices: 81.6 us -> none
    all_to_all x1 -> x0, blocking collectives: 41.9 us -> none  [on_device(): lax.all_to_all(node_sum, 'node', split_axis=1, concat_axis=1, tiled=True)]
    dot_general x4 -> x0, matrix products: 34 us -> none  [the longest x1 18.9 us: on_device(): lax.dot_general(down_rows, hidden, (((0,), (1,)), ((), ())), preferred_el...]
    all_to_all x2 -> x0, starting transfers between devices: 21.7 us -> none  [the longest x1 12 us: on_device(): lax.all_to_all(slot_gates, 'node', split_axis=0, concat_axis=0, tiled=True)]
    all_gather x1 -> x0, waiting for transfers between devices: 17.8 us -> none  [on_device(): full_rows = lax.all_gather(tokens, 'local', axis=1, tiled=True)]
    unnamed x2 -> x1, local copies, waits for them, and re-layouts: 16.5 us -> 1.65 us
  transfers between devices with their start and end apart: 4 -> 0, of which waited for: 3 -> 0; matrix products, arithmetic and copies ran while one was open for 2% -> 0% of each run, Pallas kernels for 0% -> 0%
where the time goes in v1:
time: 143 us; the launch traced here: 142 us
  Pallas kernels  141 us (99%)
  local copies, waits for them, and re-layouts  1.65 us (1%)
    pallas_call x1, Pallas kernels, on_device(): pl.pallas_call(kernel, name='routed_experts', out_shape=jax.ShapeDtypeStr...  141 us

profile of v1, /device:TPU:1, one launch (start us, length us, event | category | flops | bytes accessed | tf_op | source)
XLA Modules:
  0.0 142.4 jit_solution(12311821165162993530)
XLA Ops:
  0.0 140.7 %routed_experts.1 = bf16[128,896]{1,0:T(8,128)(2,1)} custom-call(bf16[128,896]{1,0:T(8,128)(2,1)} %tok.1, s32[8,128]{1,0:T(8,128)} %bitcast.2, bf16[8,128]{1,0:T(8,128)(2,1)} %bitcast.3, bf16[1,7168,256]{2,1,0:T(8,128)(2,1)} %wg_h.1, bf16[1,7168,256]{2,1,0:T(8,128)(2,1)} %wu_h.1, bf16[1,256,7168]{2,1,0:T(8,128)(2,1)} %wd_h.1), custom_call_target="tpu_custom_call" | custom-call | flops 8499999744 | bytes 12000000 | tf_op jit(solution)/shard_map/routed_experts/pallas_call | solution.py:350
  140.7 1.6 %copy.8 = bf16[128,896]{1,0:T(8,128)(2,1)} copy(bf16[128,896]{1,0:T(8,128)(2,1)} %routed_experts.1) | data formatting | bytes 458752

commit v2 on v0

v2 whole, which is shorter than its diff:
```python
import jax
import jax.numpy as jnp
from jax import lax
from jax.experimental import pallas as pl
from jax.experimental.pallas import tpu as pltpu
from jax.sharding import PartitionSpec as P

F32, BF16 = jnp.float32, jnp.bfloat16
NY, NZ, NX = 4, 8, 4
TOK = 128
FEAT = 896
WIDTH = 256
DEPTH = FEAT * 8
CAP = 24
PAIR = 2 * CAP
ROWS = NY * PAIR
HALF = ROWS // 2
EARLY = 256
MAIN = FEAT - EARLY
WIDE = MAIN + 4 * EARLY
GATE = 128
CHUNKS = ((0, 4), (3, 5), (2, 6), (1, 7))
SLOT = {0: 0, 4: 1, 3: 2, 5: 3, 2: 4, 6: 5, 1: 6, 7: 7}
OWN = GATE
SIB = GATE + WIDE
SIDE = GATE + 2 * WIDE
MISSING = -100.0
PARTS = ((0, 512), (512, 384))
EAGER = (0, 1)
ORDER = (
    "z1", "z2", "s2", "z3", "s0", "a4", "a5", "s1", "a0", "a1", "b5", "b4",
    "b0", "b1", "c5", "s3", "a3", "c0", "a2", "c1", "u0", "u1", "b3", "b2",
    "h1", "c4", "a6", "c3", "h0", "u5", "i1", "c2", "u3", "a7", "d1", "i0",
    "u2", "h3", "b6", "d0", "u4", "b7", "h5", "i3", "h2", "c6", "r0", "d3",
    "h4", "c7", "u6", "i5", "i2", "u7", "i4", "d2", "d5", "h6", "d4", "h7",
    "r1", "i6", "i7", "d6", "d7", "r2", "r3",
)


class Semaphores:
    def __init__(self, array):
        self.array, self.places, self.waited = array, {}, set()

    def at(self, name):
        return self.array.at[self.places.setdefault(name, len(self.places))]

    def wait(self, name, ref):
        if name not in self.waited:
            self.waited.add(name)
            pltpu.make_async_copy(ref, ref, self.at(name)).wait()


def kernel(
    tok, routes_t, gates_t, wg_h, wu_h, wd_h, out,
    zb, meta_out, meta_in, onehot, picked, rows, wg, wu, wd, hid, osend, ret, zso, zsi, own,
    send_sem, recv_sem, local_sem,
):
    node, local = lax.axis_index("node"), lax.axis_index("local")
    y, z, x, c = node // NZ, node % NZ, local // 2, local % 2

    def dev(dx=0, dc=0, dy=0, dz=0):
        yy, zz = (y + dy + NY) % NY, (z + dz + NZ) % NZ
        xx, cc = (x + dx + NX) % NX, (c + dc) % 2
        return (yy * NZ + zz, xx * 2 + cc)

    sent, came, loaded = Semaphores(send_sem), Semaphores(recv_sem), Semaphores(local_sem)

    def remote(src, dst, device, send, recv):
        pltpu.make_async_remote_copy(
            src_ref=src, dst_ref=dst, send_sem=sent.at(send), recv_sem=came.at(recv),
            device_id=device, device_id_type=pl.DeviceIdType.MESH,
        ).start()

    def load(src, dst, name):
        pltpu.make_async_copy(src, dst, loaded.at(name)).start()

    toward = 1 - 2 * c

    mine = zb.at[pl.ds(0, TOK), pl.ds(0, FEAT)]
    load(tok, mine, "tok")
    peers = (
        [dev(dx=i, dc=j) for i in range(NX) for j in range(2) if (i, j) != (0, 0)]
        + [dev(dy=i) for i in range(1, NY)]
        + [dev(dz=i) for i in range(1, NZ)]
    )
    barrier = pltpu.get_barrier_semaphore()
    for peer in peers:
        pl.semaphore_signal(barrier, inc=1, device_id=peer, device_id_type=pl.DeviceIdType.MESH)

    lane = lax.broadcasted_iota(jnp.int32, (TOK, TOK), 1)
    line = lax.broadcasted_iota(jnp.int32, (TOK, TOK), 0)
    step, kind = line // 16, line % 16
    target = ((y + kind % NY) % NY) * NZ + (z + step) % NZ
    expert = target * 2 + x // 2
    named = jnp.zeros((TOK, TOK), F32)
    weight = jnp.zeros((TOK, TOK), F32)
    routes_v, gates_v = routes_t[...], gates_t[...].astype(F32)
    for k in range(8):
        chosen = routes_v[k : k + 1, :]
        named = jnp.where(chosen // 2 == target, 1.0, named)
        weight = weight + jnp.where(chosen == expert, gates_v[k : k + 1, :], 0.0)
    before = jnp.where(line < lane, 1.0, 0.0).astype(BF16)
    earlier = jnp.dot(named.astype(BF16), before, preferred_element_type=F32)
    slots = jnp.where(named > 0.0, earlier, MISSING)
    meta = jnp.where(kind < 4, slots, jnp.where(kind < 8, weight, 0.0)).astype(BF16)
    meta_out[...] = meta
    meta_in[pl.ds(0, 16), :] = meta[0:16]

    loaded.wait("tok", mine)
    pl.semaphore_wait(barrier, len(peers))

    shared = zb.at[pl.ds(0, TOK), pl.ds(FEAT, 3 * EARLY)]
    for j, dx in enumerate((1, -1, 2)):
        remote(
            zb.at[pl.ds(0, TOK), pl.ds(MAIN, EARLY)],
            zb.at[pl.ds(0, TOK), pl.ds(FEAT + j * EARLY, EARLY)],
            dev(dx=dx), "first", "first",
        )

    def first_row(dx, dc):
        return (((x + dx + NX) % NX) * 2 + (c + dc) % 2) * FEAT

    def aligned(i):
        return pl.multiple_of(i, 128)

    def send_down(n):
        near = ((0, 1, 1), (1, 0, 2), (1, 1, 3), (-1, 0, 4), (-1, 1, 5))
        for dx, dc, place in (near, ((2, 0, 6), (2, 1, 7)))[n]:
            remote(
                wd_h.at[0, :, pl.ds(aligned(first_row(dx, dc)), FEAT)],
                wd.at[pl.ds(place * WIDTH, WIDTH), :],
                dev(dx=dx, dc=dc), "down", "down",
            )

    pieces = ((0, FEAT), (FEAT, 3 * EARLY))

    def part(i, p):
        return zb.at[pl.ds(SLOT[i] * TOK, TOK), pl.ds(*pieces[p])]

    def block_here(i):
        for p in range(2):
            came.wait(f"z{i}{p}", part(i, p))

    def hop(p, i):
        remote(part(i, p), part(i + 1, p), dev(dz=1), "z", f"z{i + 1}{p}")
        j = (8 - i) % 8
        remote(part(j, p), part(7 - i, p), dev(dz=-1), "z", f"z{7 - i}{p}")

    hop(0, 0)
    for n in EAGER:
        send_down(n)
    came.wait("first", shared)
    hop(1, 0)
    for i in range(1, NZ):
        remote(
            meta_out.at[pl.ds(16 * i, 16), :], meta_in.at[pl.ds(16 * SLOT[i], 16), :],
            dev(dz=i), "meta", "meta",
        )
    metas = meta_in.at[pl.ds(16, 16 * 7), :]

    def relay(i):
        for p in range(2):
            came.wait(f"z{i}{p}", part(i, p))
            came.wait(f"z{8 - i}{p}", part(8 - i, p))
            if i < 3:
                hop(p, i)
            else:
                source = zb.at[pl.ds((SLOT[3] + c) * TOK, TOK), pl.ds(*pieces[p])]
                remote(source, part(4, p), dev(dz=toward), "z", f"z4{p}")

    spans = []
    for dc in range(2):
        spans.append((first_row(0, dc), dc * WIDE, FEAT))
        for j, dx in enumerate((-1, 1, 2)):
            spans.append((first_row(dx, dc) + MAIN, dc * WIDE + FEAT + j * EARLY, EARLY))
    for j, dx in enumerate((-1, 1, 2)):
        for dc in range(2):
            spans.append((first_row(dx, dc), 2 * WIDE + (2 * j + dc) * MAIN, MAIN))
    for src, dst, size in spans:
        for name, hbm, vmem in (("wg", wg_h, wg), ("wu", wu_h, wu)):
            load(hbm.at[0, pl.ds(aligned(src), size), :], vmem.at[pl.ds(dst, size), :], name)
    own_down = wd.at[pl.ds(0, WIDTH), :]
    load(wd_h.at[0, :, pl.ds(aligned(first_row(0, 0)), FEAT)], own_down, "wd")

    def select(k):
        came.wait("meta", metas)
        for i in CHUNKS[k]:
            if i:
                block_here(i)
        near, far = (meta_in[pl.ds(16 * (2 * k + i), 16), :].astype(F32) for i in range(2))
        place = lax.broadcasted_iota(jnp.int32, (PAIR, 2 * TOK), 0).astype(F32)
        for j in range(NY):
            slot = jnp.concatenate([near[j : j + 1], far[j : j + 1] + CAP], axis=1)
            gate = jnp.concatenate([near[4 + j : 5 + j], far[4 + j : 5 + j]], axis=1)
            hit = jnp.where(place == slot, 1.0, 0.0)
            onehot[k, pl.ds(j * PAIR, PAIR), :] = hit.astype(BF16)
            share = jnp.sum(hit * gate, axis=1, keepdims=True)
            picked[k, pl.ds(j * PAIR, PAIR), pl.ds(0, GATE)] = jnp.broadcast_to(
                share, (PAIR, GATE)
            ).astype(BF16)
        chosen = jnp.dot(
            onehot[k], zb[pl.ds(2 * k * TOK, 2 * TOK), :], preferred_element_type=F32
        ).astype(BF16)
        picked[k, :, pl.ds(GATE, WIDE)] = chosen
        for j in range(1, NY):
            remote(
                picked.at[k, pl.ds(j * PAIR, PAIR), :],
                rows.at[k, pl.ds(j * PAIR, PAIR), pl.ds(0, GATE + WIDE)],
                dev(dy=j), f"y{k}", f"y{k}{j // 2}",
            )
        rows[k, pl.ds(0, PAIR), pl.ds(0, GATE + WIDE)] = picked[k, pl.ds(0, PAIR), :]

    def half(ref, q, first, size):
        return ref.at[q // 2, pl.ds(q % 2 * HALF, HALF), pl.ds(first, size)]

    def cols(q, first, size):
        return half(rows, q, first, size)

    def side(q, j, dc=0):
        return cols(q, SIDE + (2 * j + dc) * MAIN, MAIN)

    def sources(q):
        return (2, 3) if q % 2 else (1,)

    def rows_a(q):
        count = len(sources(q)) * PAIR
        place = pl.ds(sources(q)[0] * PAIR, count)
        came.wait(f"y{q // 2}{q % 2}", rows.at[q // 2, place, pl.ds(0, GATE + WIDE)])
        own_cols = cols(q, OWN, MAIN)
        remote(own_cols, side(q, 0), dev(dx=1), f"x{q}", f"x{q}")
        remote(own_cols, side(q, 1), dev(dx=-1), f"x{q}", f"x{q}")
        remote(cols(q, OWN, WIDE), cols(q, SIB, WIDE), dev(dc=1), f"x{q}", f"s{q}")

    def rows_b(q):
        came.wait(f"x{q}", cols(q, SIDE, 2 * MAIN))
        passed = cols(q, aligned(SIDE + c * 2 * MAIN), MAIN)
        remote(passed, side(q, 2), dev(dx=toward), f"x{q}", f"o{q}")
        for j in range(2):
            remote(side(q, j), side(q, j, 1), dev(dc=1), f"x{q}", f"s{q}")

    def rows_c(q):
        came.wait(f"o{q}", side(q, 2))
        remote(side(q, 2), side(q, 2, 1), dev(dc=1), f"x{q}", f"s{q}")

    def hcol(q, place):
        return half(hid, q, place * WIDTH, WIDTH)

    def up(q):
        came.wait(f"s{q}", cols(q, SIB, WIDE + 3 * MAIN))
        lines = pl.ds(q % 2 * HALF, HALF)
        given = rows[q // 2, lines, pl.ds(GATE, DEPTH)]
        gate_act = jnp.dot(given, wg[...], preferred_element_type=F32)
        up_act = jnp.dot(given, wu[...], preferred_element_type=F32)
        share = rows[q // 2, lines, pl.ds(0, GATE)].astype(F32)
        share = jnp.concatenate([share, share], axis=1)
        value = gate_act / (1.0 + jnp.exp(-gate_act)) * up_act * share
        hid[q // 2, lines, pl.ds(0, WIDTH)] = value.astype(BF16)
        remote(hcol(q, 0), hcol(q, 2), dev(dx=1), f"h{q}", f"h{q}")
        remote(hcol(q, 0), hcol(q, 4), dev(dx=-1), f"h{q}", f"h{q}")
        remote(hcol(q, 0), hcol(q, 1), dev(dc=1), f"h{q}", f"t{q}")

    def hid_b(q):
        came.wait(f"h{q}", half(hid, q, 2 * WIDTH, 2 * WIDTH))
        passed = half(hid, q, aligned((2 + 2 * c) * WIDTH), WIDTH)
        remote(passed, hcol(q, 6), dev(dx=toward), f"h{q}", f"p{q}")
        for j in range(2):
            remote(hcol(q, 2 + 2 * j), hcol(q, 3 + 2 * j), dev(dc=1), f"h{q}", f"t{q}")

    def hid_c(q):
        came.wait(f"p{q}", hcol(q, 6))
        remote(hcol(q, 6), hcol(q, 7), dev(dc=1), f"h{q}", f"t{q}")

    def down(q):
        came.wait(f"t{q}", half(hid, q, 0, 4 * WIDTH))
        loaded.wait("wd", own_down)
        came.wait("down", wd.at[pl.ds(WIDTH, 7 * WIDTH), :])
        k, lines = q // 2, pl.ds(q % 2 * HALF, HALF)
        for n, span in enumerate(PARTS):
            place = pl.ds(*span)
            osend[k, lines, place] = jnp.dot(
                hid[k, lines, :], wd[:, place], preferred_element_type=F32
            ).astype(BF16)
            for j in sources(q):
                remote(
                    osend.at[k, pl.ds(j * PAIR, PAIR), place],
                    ret.at[k, pl.ds(j * PAIR, PAIR), place],
                    dev(dy=-j), f"r{k}", f"r{k}{n}",
                )
        if q % 2 == 0:
            ret[k, pl.ds(0, PAIR), :] = osend[k, pl.ds(0, PAIR), :]

    def home(k):
        for n, span in enumerate(PARTS):
            place = pl.ds(*span)
            came.wait(f"r{k}{n}", ret.at[k, pl.ds(PAIR, 3 * PAIR), place])
            total = lax.dot_general(
                onehot[k], ret[k, :, place], (((0,), (0,)), ((), ())), preferred_element_type=F32
            )
            near, far = total[:TOK], total[TOK:]
            if k == 0:
                own[:, place] = near
                zso[0, :, place] = far.astype(BF16)
                remote(
                    zso.at[0, :, place], zsi.at[0, :, place], dev(dz=-toward), "q", f"q{k}{n}"
                )
                continue
            q = 2 * k - 1
            if k == 1:
                came.wait(f"q0{n}", zsi.at[0, :, place])
                come = zsi[0, :, place].astype(F32)
                near = near + jnp.where(c == 0, come, 0.0)
                far = far + jnp.where(c == 1, come, 0.0)
            else:
                came.wait(f"q{k - 1}{n}", zsi.at[pl.ds(q - 2, 2), :, place])
                near = near + zsi[q - 2, :, place].astype(F32)
                far = far + zsi[q - 1, :, place].astype(F32)
            zso[q, :, place] = near.astype(BF16)
            zso[q + 1, :, place] = far.astype(BF16)
            remote(zso.at[q, :, place], zsi.at[q, :, place], dev(dz=-1), "q", f"q{k}{n}")
            remote(zso.at[q + 1, :, place], zsi.at[q + 1, :, place], dev(dz=1), "q", f"q{k}{n}")

    steps = {
        "z": relay, "s": select, "a": rows_a, "b": rows_b, "c": rows_c, "u": up, "h": hid_b,
        "i": hid_c, "d": down, "r": home, "w": send_down,
    }
    for step in ORDER:
        if step[0] == "u":
            loaded.wait("wg", wg)
            loaded.wait("wu", wu)
        steps[step[0]](int(step[1]))
    for n, span in enumerate(PARTS):
        place = pl.ds(*span)
        came.wait(f"q3{n}", zsi.at[pl.ds(5, 2), :, place])
        total = own[:, place] + zsi[5, :, place].astype(F32) + zsi[6, :, place].astype(F32)
        out[:, place] = total.astype(BF16)

    sent.wait("first", shared)
    sent.wait("z", zb.at[pl.ds(TOK, 7 * TOK), :])
    sent.wait("meta", metas)
    sent.wait("down", wd.at[pl.ds(WIDTH, 7 * WIDTH), :])
    for k in range(4):
        sent.wait(f"y{k}", picked.at[k, pl.ds(PAIR, 3 * PAIR), :])
        sent.wait(f"r{k}", osend.at[k, pl.ds(PAIR, 3 * PAIR), :])
    for q in range(8):
        sent.wait(f"x{q}", cols(q, SIB, WIDE + 6 * MAIN))
        sent.wait(f"h{q}", half(hid, q, WIDTH, 7 * WIDTH))
    sent.wait("q", zso)


def on_device(tokens, routes, gates, w_gate, w_up, w_down):
    any_spec = pl.BlockSpec(memory_space=pl.ANY)
    vmem_spec = pl.BlockSpec(memory_space=pltpu.VMEM)
    return pl.pallas_call(
        kernel,
        name="routed_experts",
        out_shape=jax.ShapeDtypeStruct((TOK, FEAT), BF16),
        in_specs=[any_spec, vmem_spec, vmem_spec, any_spec, any_spec, any_spec],
        out_specs=vmem_spec,
        scratch_shapes=[
            pltpu.VMEM((NZ * TOK, WIDE), BF16),
            pltpu.VMEM((NZ * 16, TOK), BF16),
            pltpu.VMEM((NZ * 16, TOK), BF16),
            pltpu.VMEM((4, ROWS, 2 * TOK), BF16),
            pltpu.VMEM((4, ROWS, GATE + WIDE), BF16),
            pltpu.VMEM((4, ROWS, GATE + DEPTH), BF16),
            pltpu.VMEM((DEPTH, WIDTH), BF16),
            pltpu.VMEM((DEPTH, WIDTH), BF16),
            pltpu.VMEM((8 * WIDTH, FEAT), BF16),
            pltpu.VMEM((4, ROWS, 8 * WIDTH), BF16),
            pltpu.VMEM((4, ROWS, FEAT), BF16),
            pltpu.VMEM((4, ROWS, FEAT), BF16),
            pltpu.VMEM((7, TOK, FEAT), BF16),
            pltpu.VMEM((7, TOK, FEAT), BF16),
            pltpu.VMEM((TOK, FEAT), F32),
            pltpu.SemaphoreType.DMA((29,)),
            pltpu.SemaphoreType.DMA((89,)),
            pltpu.SemaphoreType.DMA((4,)),
        ],
        compiler_params=pltpu.CompilerParams(
            collective_id=0, has_side_effects=True, vmem_limit_bytes=56 << 20
        ),
        cost_estimate=pl.CostEstimate(
            flops=8_500_000_000, bytes_accessed=12_000_000, transcendentals=200_000
        ),
    )(tokens, routes.T, gates.T, w_gate, w_up, w_down)


def solution(mesh):
    return jax.shard_map(
        on_device,
        mesh=mesh,
        in_specs=(
            P("node", "local"),
            P("node", None),
            P("node", None),
            P(("node", "local"), None, None),
            P(("node", "local"), None, None),
            P(("node", "local"), None, None),
        ),
        out_specs=P("node", "local"),
        check_vma=False,
    )
```

time: 480 us -> 123 us (0.26)
  waiting for transfers between devices: 345 us -> 0 us
  Pallas kernels: 0 us -> 121 us
  blocking collectives: 41.9 us -> 0 us
  matrix products: 34 us -> 0 us
  starting transfers between devices: 21.8 us -> 0 us
  local copies, waits for them, and re-layouts: 16.9 us -> 1.65 us
  between operations: 13.5 us -> 0.01 us
    all_to_all x2 -> x0, waiting for transfers between devices: 245 us -> none  [the longest x1 245 us: on_device(): lax.all_to_all(outgoing, 'node', split_axis=0, concat_axis=0, tiled=True)]
    pallas_call x0 -> x1, Pallas kernels: none -> 121 us  [on_device(): pl.pallas_call(kernel, name='routed_experts', out_shape=jax.ShapeDtypeStr...]
    unnamed x3 -> x0, waiting for transfers between devices: 81.6 us -> none
    all_to_all x1 -> x0, blocking collectives: 41.9 us -> none  [on_device(): lax.all_to_all(node_sum, 'node', split_axis=1, concat_axis=1, tiled=True)]
    dot_general x4 -> x0, matrix products: 34 us -> none  [the longest x1 18.9 us: on_device(): lax.dot_general(down_rows, hidden, (((0,), (1,)), ((), ())), preferred_el...]
    all_to_all x2 -> x0, starting transfers between devices: 21.7 us -> none  [the longest x1 12 us: on_device(): lax.all_to_all(slot_gates, 'node', split_axis=0, concat_axis=0, tiled=True)]
    all_gather x1 -> x0, waiting for transfers between devices: 17.8 us -> none  [on_device(): full_rows = lax.all_gather(tokens, 'local', axis=1, tiled=True)]
    unnamed x2 -> x1, local copies, waits for them, and re-layouts: 16.5 us -> 1.65 us
  transfers between devices with their start and end apart: 4 -> 0, of which waited for: 3 -> 0; matrix products, arithmetic and copies ran while one was open for 2% -> 0% of each run, Pallas kernels for 0% -> 0%
where the time goes in v2:
time: 123 us
  Pallas kernels  121 us (98%)
  local copies, waits for them, and re-layouts  1.65 us (1%)
    pallas_call x1, Pallas kernels, on_device(): pl.pallas_call(kernel, name='routed_experts', out_shape=jax.ShapeDtypeStr...  121 us

profile of v2, /device:TPU:1, one launch (start us, length us, event | category | flops | bytes accessed | tf_op | source)
XLA Modules:
  0.0 122.9 jit_solution(3416952470256256316)
XLA Ops:
  0.0 121.3 %routed_experts.1 = bf16[128,896]{1,0:T(8,128)(2,1)} custom-call(bf16[128,896]{1,0:T(8,128)(2,1)} %tok.1, s32[8,128]{1,0:T(8,128)} %bitcast.2, bf16[8,128]{1,0:T(8,128)(2,1)} %bitcast.3, bf16[1,7168,256]{2,1,0:T(8,128)(2,1)} %wg_h.1, bf16[1,7168,256]{2,1,0:T(8,128)(2,1)} %wu_h.1, bf16[1,256,7168]{2,1,0:T(8,128)(2,1)} %wd_h.1), custom_call_target="tpu_custom_call" | custom-call | flops 8499999744 | bytes 12000000 | tf_op jit(solution)/shard_map/routed_experts/pallas_call | solution.py:353
  121.3 1.6 %copy.8 = bf16[128,896]{1,0:T(8,128)(2,1)} copy(bf16[128,896]{1,0:T(8,128)(2,1)} %routed_experts.1) | data formatting | bytes 458752

commit v3 on v2

--- a/solution.py
+++ b/solution.py
@@ -25,15 +25,22 @@
 SIB = GATE + WIDE
 SIDE = GATE + 2 * WIDE
 MISSING = -100.0
-PARTS = ((0, 512), (512, 384))
-EAGER = (0, 1)
+PARTS = ((0, 384), (384, 256), (640, 256))
+EAGER = (0,)
+DIRECT = (6, 7)
+DOWN = (
+    ((0, 1, 1), (1, 0, 2), (-1, 0, 4)),
+    ((1, 1, 3), (-1, 1, 5)),
+    ((2, 0, 6),),
+    ((2, 1, 7),),
+)
 ORDER = (
-    "z1", "z2", "s2", "z3", "s0", "a4", "a5", "s1", "a0", "a1", "b5", "b4",
-    "b0", "b1", "c5", "s3", "a3", "c0", "a2", "c1", "u0", "u1", "b3", "b2",
-    "h1", "c4", "a6", "c3", "h0", "u5", "i1", "c2", "u3", "a7", "d1", "i0",
-    "u2", "h3", "b6", "d0", "u4", "b7", "h5", "i3", "h2", "c6", "r0", "d3",
-    "h4", "c7", "u6", "i5", "i2", "u7", "i4", "d2", "d5", "h6", "d4", "h7",
-    "r1", "i6", "i7", "d6", "d7", "r2", "r3",
+    "z1", "w3", "w2", "z2", "s2", "z3", "s1", "w1", "a2", "s0", "a4", "a0",
+    "a3", "a1", "b0", "s3", "b3", "a5", "b1", "b2", "c0", "b4", "u0", "c3",
+    "a6", "c1", "u1", "h0", "b5", "u3", "c2", "c4", "h1", "b6", "u2", "h3",
+    "c5", "i1", "a7", "u4", "d1", "h2", "i0", "u5", "i3", "d0", "b7", "c6",
+    "d3", "h4", "i2", "h5", "u6", "c7", "r0", "d2", "i4", "i5", "u7", "h6",
+    "d5", "r1", "i6", "d4", "h7", "i7", "d6", "d7", "r2", "r3",
 )
 
 
@@ -56,11 +63,22 @@
     send_sem, recv_sem, local_sem,
 ):
     node, local = lax.axis_index("node"), lax.axis_index("local")
-    y, z, x, c = node // NZ, node % NZ, local // 2, local % 2
+    y, z = lax.div(node, NZ), lax.rem(node, NZ)
+    x, c = lax.div(local, 2), lax.rem(local, 2)
+
+    devices = {}
 
     def dev(dx=0, dc=0, dy=0, dz=0):
-        yy, zz = (y + dy + NY) % NY, (z + dz + NZ) % NZ
-        xx, cc = (x + dx + NX) % NX, (c + dc) % 2
+        if not isinstance(dx, int) or not isinstance(dz, int):
+            return place_of(dx, dc, dy, dz)
+        key = (dx % NX, dc, dy % NY, dz % NZ)
+        if key not in devices:
+            devices[key] = place_of(*key)
+        return devices[key]
+
+    def place_of(dx, dc, dy, dz):
+        yy, zz = lax.rem(y + dy + NY, NY), lax.rem(z + dz + NZ, NZ)
+        xx, cc = lax.rem(x + dx + NX, NX), lax.rem(c + dc, 2)
         return (yy * NZ + zz, xx * 2 + cc)
 
     sent, came, loaded = Semaphores(send_sem), Semaphores(recv_sem), Semaphores(local_sem)
@@ -87,17 +105,59 @@
     for peer in peers:
         pl.semaphore_signal(barrier, inc=1, device_id=peer, device_id_type=pl.DeviceIdType.MESH)
 
+    pl.semaphore_wait(barrier, len(peers))
+
+    shared = zb.at[pl.ds(0, TOK), pl.ds(FEAT, 3 * EARLY)]
+    for j, dx in enumerate((1, -1, 2)):
+        remote(
+            tok.at[:, pl.ds(MAIN, EARLY)],
+            zb.at[pl.ds(0, TOK), pl.ds(FEAT + j * EARLY, EARLY)],
+            dev(dx=dx), "first", "first",
+        )
+
+    def first_row(dx, dc):
+        return (((x + dx + NX) % NX) * 2 + (c + dc) % 2) * FEAT
+
+    def aligned(i):
+        return pl.multiple_of(i, 128)
+
+    def send_down(n):
+        for dx, dc, place in DOWN[n]:
+            remote(
+                wd_h.at[0, :, pl.ds(aligned(first_row(dx, dc)), FEAT)],
+                wd.at[pl.ds(place * WIDTH, WIDTH), :],
+                dev(dx=dx, dc=dc), "down", "down",
+            )
+
+    pieces = ((0, FEAT), (FEAT, 3 * EARLY))
+
+    def part(i, p):
+        return zb.at[pl.ds(SLOT[i] * TOK, TOK), pl.ds(*pieces[p])]
+
+    def block_here(i):
+        for p in range(2):
+            came.wait(f"z{i}{p}", part(i, p))
+
+    def hop(p, i):
+        remote(part(i, p), part(i + 1, p), dev(dz=1), "z", f"z{i + 1}{p}")
+        j = (8 - i) % 8
+        remote(part(j, p), part(7 - i, p), dev(dz=-1), "z", f"z{7 - i}{p}")
+
+    remote(tok, part(1, 0), dev(dz=1), "z", "z10")
+    remote(tok, part(7, 0), dev(dz=-1), "z", "z70")
+    for n in EAGER:
+        send_down(n)
     lane = lax.broadcasted_iota(jnp.int32, (TOK, TOK), 1)
     line = lax.broadcasted_iota(jnp.int32, (TOK, TOK), 0)
-    step, kind = line // 16, line % 16
-    target = ((y + kind % NY) % NY) * NZ + (z + step) % NZ
+    step, kind = line >> 4, line & 15
+    target = ((y + kind) & (NY - 1)) * NZ + ((z + step) & (NZ - 1))
     expert = target * 2 + x // 2
     named = jnp.zeros((TOK, TOK), F32)
     weight = jnp.zeros((TOK, TOK), F32)
     routes_v, gates_v = routes_t[...], gates_t[...].astype(F32)
     for k in range(8):
         chosen = routes_v[k : k + 1, :]
-        named = jnp.where(chosen // 2 == target, 1.0, named)
+        named = jnp.where(chosen >> 1 == target, 1.0, named)
         weight = weight + jnp.where(chosen == expert, gates_v[k : k + 1, :], 0.0)
     before = jnp.where(line < lane, 1.0, 0.0).astype(BF16)
     earlier = jnp.dot(named.astype(BF16), before, preferred_element_type=F32)
@@ -106,51 +166,9 @@
     meta_out[...] = meta
     meta_in[pl.ds(0, 16), :] = meta[0:16]
 
-    loaded.wait("tok", mine)
-    pl.semaphore_wait(barrier, len(peers))
-
-    shared = zb.at[pl.ds(0, TOK), pl.ds(FEAT, 3 * EARLY)]
-    for j, dx in enumerate((1, -1, 2)):
-        remote(
-            zb.at[pl.ds(0, TOK), pl.ds(MAIN, EARLY)],
-            zb.at[pl.ds(0, TOK), pl.ds(FEAT + j * EARLY, EARLY)],
-            dev(dx=dx), "first", "first",
-        )
-
-    def first_row(dx, dc):
-        return (((x + dx + NX) % NX) * 2 + (c + dc) % 2) * FEAT
-
-    def aligned(i):
-        return pl.multiple_of(i, 128)
-
-    def send_down(n):
-        near = ((0, 1, 1), (1, 0, 2), (1, 1, 3), (-1, 0, 4), (-1, 1, 5))
-        for dx, dc, place in (near, ((2, 0, 6), (2, 1, 7)))[n]:
-            remote(
-                wd_h.at[0, :, pl.ds(aligned(first_row(dx, dc)), FEAT)],
-                wd.at[pl.ds(place * WIDTH, WIDTH), :],
-                dev(dx=dx, dc=dc), "down", "down",
-            )
-
-    pieces = ((0, FEAT), (FEAT, 3 * EARLY))
-
-    def part(i, p):
-        return zb.at[pl.ds(SLOT[i] * TOK, TOK), pl.ds(*pieces[p])]
-
-    def block_here(i):
-        for p in range(2):
-            came.wait(f"z{i}{p}", part(i, p))
-
-    def hop(p, i):
-        remote(part(i, p), part(i + 1, p), dev(dz=1), "z", f"z{i + 1}{p}")
-        j = (8 - i) % 8
-        remote(part(j, p), part(7 - i, p), dev(dz=-1), "z", f"z{7 - i}{p}")
-
-    hop(0, 0)
-    for n in EAGER:
-        send_down(n)
     came.wait("first", shared)
     hop(1, 0)
+    loaded.wait("tok", mine)
     for i in range(1, NZ):
         remote(
             meta_out.at[pl.ds(16 * i, 16), :], meta_in.at[pl.ds(16 * SLOT[i], 16), :],
@@ -257,12 +275,15 @@
         hid[q // 2, lines, pl.ds(0, WIDTH)] = value.astype(BF16)
         remote(hcol(q, 0), hcol(q, 2), dev(dx=1), f"h{q}", f"h{q}")
         remote(hcol(q, 0), hcol(q, 4), dev(dx=-1), f"h{q}", f"h{q}")
+        if q in DIRECT:
+            remote(hcol(q, 0), hcol(q, 6), dev(dx=2), f"h{q}", f"p{q}")
         remote(hcol(q, 0), hcol(q, 1), dev(dc=1), f"h{q}", f"t{q}")
 
     def hid_b(q):
         came.wait(f"h{q}", half(hid, q, 2 * WIDTH, 2 * WIDTH))
-        passed = half(hid, q, aligned((2 + 2 * c) * WIDTH), WIDTH)
-        remote(passed, hcol(q, 6), dev(dx=toward), f"h{q}", f"p{q}")
+        if q not in DIRECT:
+            passed = half(hid, q, aligned((2 + 2 * c) * WIDTH), WIDTH)
+            remote(passed, hcol(q, 6), dev(dx=toward), f"h{q}", f"p{q}")
         for j in range(2):
             remote(hcol(q, 2 + 2 * j), hcol(q, 3 + 2 * j), dev(dc=1), f"h{q}", f"t{q}")
 
@@ -373,7 +394,7 @@
             pltpu.VMEM((7, TOK, FEAT), BF16),
             pltpu.VMEM((TOK, FEAT), F32),
             pltpu.SemaphoreType.DMA((29,)),
-            pltpu.SemaphoreType.DMA((89,)),
+            pltpu.SemaphoreType.DMA((97,)),
             pltpu.SemaphoreType.DMA((4,)),
         ],
         compiler_params=pltpu.CompilerParams(

time: 123 us -> 121 us (0.984)
    pallas_call x1, Pallas kernels: 121 us -> 120 us  [on_device(): pl.pallas_call(kernel, name='routed_experts', out_shape=jax.ShapeDtypeStr...]
where the time goes in v3:
time: 121 us
  Pallas kernels  120 us (99%)
  local copies, waits for them, and re-layouts  1.65 us (1%)
    pallas_call x1, Pallas kernels, on_device(): pl.pallas_call(kernel, name='routed_experts', out_shape=jax.ShapeDtypeStr...  120 us

profile of v3, /device:TPU:1, one launch (start us, length us, event | category | flops | bytes accessed | tf_op | source)
XLA Modules:
  0.0 121.2 jit_solution(4977015962403465050)
XLA Ops:
  0.0 119.6 %routed_experts.1 = bf16[128,896]{1,0:T(8,128)(2,1)} custom-call(bf16[128,896]{1,0:T(8,128)(2,1)} %tok.1, s32[8,128]{1,0:T(8,128)} %bitcast.2, bf16[8,128]{1,0:T(8,128)(2,1)} %bitcast.3, bf16[1,7168,256]{2,1,0:T(8,128)(2,1)} %wg_h.1, bf16[1,7168,256]{2,1,0:T(8,128)(2,1)} %wu_h.1, bf16[1,256,7168]{2,1,0:T(8,128)(2,1)} %wd_h.1), custom_call_target="tpu_custom_call" | custom-call | flops 8499999744 | bytes 12000000 | tf_op jit(solution)/shard_map/routed_experts/pallas_call | solution.py:374
  119.6 1.6 %copy.8 = bf16[128,896]{1,0:T(8,128)(2,1)} copy(bf16[128,896]{1,0:T(8,128)(2,1)} %routed_experts.1) | data formatting | bytes 458752
